TPU v7x, 32 devices: a whole 2x2x4 slice. The times are simulated.
32 devices in a mesh: row: 4 (over y, core), col: 8 (over z, x).
Axes of the slice: x: 2, y: 2, z: 4, core: 2. Of those that a mesh axis runs over, the one named last changes fastest.
Arguments:
- features: bfloat16 [32768, 128], P('col', 'row'), may hold values from -6 to 6
- block_codes: int32 [4, 3072], P('row', 'col'), may hold values from 0 to 8191
- block_count: int32 [4, 8], P('row', 'col'), may hold values from 1 to 384, as said below
- block_values: bfloat16 [4, 3072, 4096], P('row', 'col'), may hold values from -0.119628906 to 0.119628906
- weight: bfloat16 [128, 256], replicated, may hold values from -0.5 to 0.5
- bias: float32 [256], replicated, may hold values from -3 to 3
Outputs:
- activated: bfloat16 [32768, 256], P(('row', 'col'))
Inputs may be any that keep to these rules, and one draw needn't show every extreme that they name: `block_count`: every tile's count is at most 384; some tile holds exactly 384 in every draw; counts are skewed, the busiest tile about three times the mean. `block_codes`: A code c names local row block c // 64 and local column block c % 64.
All inputs are finite; a program needn't handle non-finite values.
Results may differ from a plain program's by a relative error of at most 0.0045.
Values may be sent and summed in bfloat16 or wider, within the bound.
No kernel may reach another device: no remote copies, remote signals or barrier semaphores. Data moves between devices by JAX's collectives and lax.ppermute only.
A program may use at most 128 MiB of HBM per device.

v0:
```python
import jax
import jax.numpy as jnp
from jax import lax
from jax.sharding import PartitionSpec as P

BLK = 64


def shards(features, block_codes, block_count, block_values, weight, bias):
    width = features.shape[1] * lax.axis_size("row")
    slab = lax.all_gather(features, "row", axis=1, tiled=True)
    col_blocks = slab.shape[0] // BLK
    row_total = col_blocks * lax.axis_size("col") // lax.axis_size("row")
    slots = block_codes.shape[1]
    tile_codes = block_codes[0]
    row_block = tile_codes // col_blocks
    col_block = tile_codes % col_blocks
    is_live = jnp.arange(slots, dtype=jnp.int32) < block_count[0, 0]
    picked = slab.reshape(col_blocks, BLK, width)[col_block]
    blocks = block_values[0].reshape(slots, BLK, BLK)
    products = jnp.einsum("bij,bjf->bif", blocks, picked, preferred_element_type=jnp.float32)
    products = jnp.where(is_live[:, None, None], products, jnp.zeros_like(products))
    partial_rows = jax.ops.segment_sum(products, row_block, num_segments=row_total)
    partial_rows = partial_rows.reshape(row_total * BLK, width)
    summed = lax.psum_scatter(partial_rows, "col", scatter_dimension=0, tiled=True)
    aggregated = summed.astype(jnp.bfloat16)
    hidden = jnp.dot(aggregated, weight, preferred_element_type=jnp.float32) + bias
    return jnp.maximum(hidden, 0.0).astype(jnp.bfloat16)


def solution(mesh):
    in_specs = (P("col", "row"), P("row", "col"), P("row", "col"), P("row", "col", None), P(), P())
    out_specs = P(("row", "col"), None)
    return jax.shard_map(shards, mesh=mesh, in_specs=in_specs, out_specs=out_specs, check_vma=False)
```

profile of v0, /device:TPU:0, one launch (start us, length us, event | category | flops | bytes accessed | tf_op | source)
XLA Modules:
  0.0 213.8 jit_solution(13100208605468430075)
XLA Ops:
  6.5 0.0 copy-start
  6.5 0.0 all-gather.2.cloned.1.call-start
  6.5 0.7 all-gather.2.cloned.1.call-update
  7.3 0.0 reduce-scatter.2.cloned.1.call-start
  7.3 3.4 %copy.11 = bf16[1,384,4096]{1,2,0:T(8,128)(2,1)S(1)} copy(bf16[1,384,4096]{2,1,0:T(8,128)(2,1)} %param.9) | data formatting | bytes 6291456 | tf_op args[3]
  10.7 0.0 copy-start.1
  10.8 9.6 %copy.12 = bf16[384,64,64]{2,1,0:T(8,128)(2,1)} copy(bf16[384,64,64]{0,2,1:T(8,128)(2,1)S(1)} %bitcast.29) | data formatting | bytes 6291456 | tf_op jit(solution)/shard_map/reshape;squeeze | solution.py:20
  21.0 0.0 copy-done.1
  21.0 7.3 %all-gather.2.cloned.1.call-done = bf16[4096,128]{0,1:T(8,128)(2,1)} async-done(((bf16[4096,32]{0,1:T(8,128)(2,1)}), bf16[4096,128]{0,1:T(8,128)(2,1)}) %all-gather.2.cloned.1.call-update) | async-done | bytes 1048592 | tf_op jit(solution)/shard_map/all_gather | solution.py:11
  28.4 1.6 copy.10
  30.0 13.3 %gather_fusion = bf16[384,64,128]{2,1,0:T(8,128)(2,1)} fusion(bf16[64,64,128]{2,1,0:T(8,128)(2,1)S(1)} %bitcast.28, s32[1024]{0:T(1024)S(1)} %pad_clamp_fusion), kind=kCustom, calls=%fused_computation | custom fusion | bytes 12584448 | tf_op jit(solution)/shard_map/gather | solution.py:19
  43.3 11.0 %select_bitcast_fusion = f32[384,64,128]{2,1,0:T(8,128)} fusion(pred[384]{0:T(512)(128)(4,1)S(1)} %iota_compare_fusion, bf16[384,64,64]{2,1,0:T(8,128)(2,1)} %copy.12, bf16[384,64,128]{2,1,0:T(8,128)(2,1)} %gather_fusion), kind=kOutput, calls=%fused_computation.2 | convolution fusion | flops 405798912 | bytes 22020480 | tf_op jit(solution)/shard_map/bij,bjf->bif/dot_general | solution.py:21
  54.3 2.5 %broadcast_in_dim.18 = f32[128,64,128]{2,1,0:T(8,128)} broadcast(f32[]{:T(128)} %constant.27.clone.1), dimensions={} | broadcast | bytes 4194308 | tf_op jit(solution)/shard_map/broadcast_in_dim | solution.py:23
  56.8 0.0 copy-start.2
  56.8 59.3 %scatter_fusion = f32[128,64,128]{2,1,0:T(8,128)} fusion(f32[128,64,128]{2,1,0:T(8,128)} %broadcast_in_dim.18, s32[384]{0:T(512)S(1)} %get-tuple-element.6, f32[384,64,128]{2,1,0:T(8,128)} %select_bitcast_fusion), kind=kCustom, calls=%fused_computation.1 | custom fusion | flops 3145728 | bytes 37750272 | tf_op jit(solution)/shard_map/scatter-add | solution.py:23
  116.1 0.0 reduce-scatter.2.cloned.1.call-update
  116.2 88.7 %reduce-scatter.2.cloned.1.call-done = f32[1024,128]{1,0:T(8,128)} async-done(((f32[8192,128]{1,0:T(8,128)}), f32[1024,128]{1,0:T(8,128)}) %reduce-scatter.2.cloned.1.call-update) | async-done | bytes 524304 | tf_op jit(solution)/shard_map/reduce_scatter | solution.py:25
  204.8 0.0 copy-done
  204.8 0.0 copy-done.2
  204.8 2.1 fusion.1
  (3 shorter events, 0.0 us)
Async XLA Ops:
  6.5 198.3 %copy-start = (bf16[128,256]{1,0:T(8,128)(2,1)S(1)}, bf16[128,256]{1,0:T(8,128)(2,1)}, u32[]{:S(2)}) copy-start(bf16[128,256]{1,0:T(8,128)(2,1)} %param.10) | copy-start | bytes 196612
  6.5 21.8 %all-gather.2.cloned.1.call-start = ((), (), s32[]{:S(2)}) async-start(), calls=%async_computation.1 | async-start | bytes 1310720 | tf_op jit(solution)/shard_map/all_gather | solution.py:11
  7.3 197.6 %reduce-scatter.2.cloned.1.call-start = ((), (), s32[]{:S(2)}) async-start(), calls=%async_computation.2 | async-start | bytes 4718592 | tf_op jit(solution)/shard_map/reduce_scatter | solution.py:25
  10.7 10.2 %copy-start.1 = (s32[1,384]{1,0:T(1,128)S(1)}, s32[1,384]{1,0:T(1,128)}, u32[]{:S(2)}) copy-start(s32[1,384]{1,0:T(1,128)} %param.7) | copy-start | bytes 4612
  56.8 148.0 %copy-start.2 = (f32[256]{0:T(256)S(1)}, f32[256]{0:T(256)}, u32[]{:S(2)}) copy-start(f32[256]{0:T(256)} %param.11) | copy-start | bytes 3076
Sparse Core Ops, SparseCore 0:
  8.9 19.4 all-gather.1
  116.3 88.5 reduce-scatter.1
where the time goes:
time: 215 us; the launch traced here: 214 us
  waiting for transfers between devices  96.7 us (45%)
  other arithmetic  59.4 us (28%)
  local copies, waits for them, and re-layouts  30.4 us (14%)
  between operations  14.1 us (7%)
  matrix products  13.1 us (6%)
    reduce_scatter x1, waiting for transfers between devices, shards(): lax.psum_scatter(partial_rows, 'col', scatter_dimension=0, tiled=True)  88.7 us
    scatter-add x1, other arithmetic, shards(): jax.ops.segment_sum(products, row_block, num_segments=row_total)  59.3 us
    gather x1, local copies, waits for them, and re-layouts, shards(): picked = slab.reshape(col_blocks, BLK, width)[col_block]  13.3 us
    dot_general x1, matrix products, shards(): jnp.einsum('bij,bjf->bif', blocks, picked, preferred_element_type=jnp.flo...  11 us
    another operation x1, local copies, waits for them, and re-layouts, shards(): blocks = block_values[0].reshape(slots, BLK, BLK)  9.56 us
    all_gather x1, waiting for transfers between devices, shards(): slab = lax.all_gather(features, 'row', axis=1, tiled=True)  7.34 us
  transfers between devices with their start and end apart: 2, of which 2 were waited for; matrix products, arithmetic and copies ran while one was open for 6% of the time, Pallas kernels for 0%

commit v1 on v0

v1 whole, which is shorter than its diff:
```python
import functools

import jax
import jax.numpy as jnp
from jax import lax
from jax.experimental import pallas as pl
from jax.experimental.pallas import tpu as pltpu
from jax.sharding import PartitionSpec as P

BLK = 64
PAIR = BLK // 2
LANES = 2 * BLK
GROUP = 16
UNROLL = 8


def relayout_kernel(values_ref, out_ref, scratch):
    for p in range(PAIR):
        scratch[p * GROUP : (p + 1) * GROUP, :] = values_ref[:, p * LANES : (p + 1) * LANES].astype(jnp.float32)
    for s in range(GROUP):
        rows = scratch[pl.ds(s, PAIR, stride=GROUP), :]
        out_ref[s * PAIR : (s + 1) * PAIR, :] = rows.astype(out_ref.dtype)


def relayout(values):
    slots = values.shape[0]
    return pl.pallas_call(
        relayout_kernel,
        grid=(slots // GROUP,),
        in_specs=[pl.BlockSpec((GROUP, BLK * BLK), lambda i: (i, 0))],
        out_specs=pl.BlockSpec((GROUP * PAIR, LANES), lambda i: (i, 0)),
        out_shape=jax.ShapeDtypeStruct((slots * PAIR, LANES), values.dtype),
        scratch_shapes=[pltpu.VMEM((GROUP * PAIR, LANES), jnp.float32)],
        cost_estimate=pl.CostEstimate(flops=0, bytes_accessed=4 * slots * BLK * BLK, transcendentals=0),
        name="relayout",
    )(values)


def product_kernel(count_ref, source_ref, target_ref, blocks_ref, ft_ref, keep_ref, send_ref, table, acc):
    lane = lax.broadcasted_iota(jnp.int32, (BLK, LANES), 1)
    low = lane < BLK

    def build(q, carry):
        x = ft_ref[:, pl.ds(pl.multiple_of(q * LANES, LANES), LANES)].astype(jnp.float32)
        both = jnp.concatenate([x, x], axis=0).T
        base = pl.multiple_of(q * 2 * LANES, 2 * LANES)
        zero = jnp.zeros((BLK, LANES), jnp.float32)
        for h in range(2):
            part = both[h * BLK : (h + 1) * BLK, :]
            full = jnp.concatenate([jnp.where(low, part, zero), jnp.where(low, zero, part)], axis=0)
            table[pl.ds(base + h * LANES, LANES), :] = full.astype(table.dtype)
        return carry

    lax.fori_loop(0, ft_ref.shape[1] // LANES, build, 0)
    acc[...] = jnp.zeros_like(acc)
    groups = (count_ref[0, 0] + (UNROLL - 1)) // UNROLL

    def step(g, carry):
        products = []
        for u in range(UNROLL):
            s = g * UNROLL + u
            block = blocks_ref[pl.ds(pl.multiple_of(s * PAIR, PAIR), PAIR), :]
            right = table[pl.ds(pl.multiple_of(source_ref[0, s], LANES), LANES), :]
            products.append(jnp.dot(block, right, preferred_element_type=jnp.float32))
        for u in range(UNROLL):
            rows = pl.ds(pl.multiple_of(target_ref[0, g * UNROLL + u], PAIR), PAIR)
            acc[rows, :] = acc[rows, :] + products[u]
        return carry

    lax.fori_loop(0, groups, step, 0)
    half = keep_ref.shape[0]
    keep_ref[...] = acc[:half, :]
    send_ref[...] = acc[half : 2 * half, :].astype(send_ref.dtype)


def product(count, source, target, blocks, ft, row_total):
    nodes = ft.shape[1]
    half = row_total // 2 * PAIR
    smem = pl.BlockSpec(memory_space=pltpu.SMEM)
    vmem = pl.BlockSpec(memory_space=pltpu.VMEM)
    return pl.pallas_call(
        product_kernel,
        in_specs=[smem, smem, smem, vmem, vmem],
        out_specs=(vmem, vmem),
        out_shape=(
            jax.ShapeDtypeStruct((half, LANES), jnp.float32),
            jax.ShapeDtypeStruct((half, LANES), jnp.bfloat16),
        ),
        scratch_shapes=[
            pltpu.VMEM((nodes * 2, LANES), jnp.bfloat16),
            pltpu.VMEM(((row_total + 1) * PAIR, LANES), jnp.float32),
        ],
        compiler_params=pltpu.CompilerParams(vmem_limit_bytes=32 * 1024 * 1024),
        cost_estimate=pl.CostEstimate(
            flops=2 * blocks.shape[0] * LANES * LANES, bytes_accessed=6 * 1024 * 1024, transcendentals=0
        ),
        name="product",
    )(count, source, target, blocks, ft)


def layer_kernel(keep0, got0, keep1, got1, even_ref, odd_ref, bias_ref, out_ref, left, right):
    first = (keep0[...] + got0[...].astype(jnp.float32)).astype(jnp.bfloat16)
    second = (keep1[...] + got1[...].astype(jnp.float32)).astype(jnp.bfloat16)
    both = jnp.concatenate([first, second], axis=1)
    rows = both.shape[0]
    for h, w_ref in enumerate((even_ref, odd_ref)):
        hidden = jnp.dot(both, w_ref[...], preferred_element_type=jnp.float32) + bias_ref[...]
        hidden = jnp.maximum(hidden, 0.0)
        left[pl.ds(h, rows, stride=2), :] = hidden[:, :LANES]
        right[pl.ds(h, rows, stride=2), :] = hidden[:, LANES:]
    out_ref[:, :LANES] = left[...].astype(out_ref.dtype)
    out_ref[:, LANES:] = right[...].astype(out_ref.dtype)


def layer(keep0, got0, keep1, got1, even, odd, bias):
    rows = keep0.shape[0]
    return pl.pallas_call(
        layer_kernel,
        out_shape=jax.ShapeDtypeStruct((2 * rows, even.shape[1]), jnp.bfloat16),
        scratch_shapes=[pltpu.VMEM((2 * rows, LANES), jnp.float32)] * 2,
        name="layer",
    )(keep0, got0, keep1, got1, even, odd, bias)


def bits_of(size):
    return range(size.bit_length() - 1)


def exchange(x, axis, size, bit):
    return lax.ppermute(x, axis, [(i, i ^ (1 << bit)) for i in range(size)])


def shards(n_row, n_col, features, block_codes, block_count, block_values, weight, bias):
    r, c = lax.axis_index("row"), lax.axis_index("col")
    top = n_row.bit_length() - 2
    low_bits, col_bits = list(range(top)), list(bits_of(n_col))

    def spread(piece):
        for bit in low_bits:
            piece = jnp.concatenate([piece, exchange(piece, "row", n_row, bit)], axis=0)
        return piece

    mine = features.T
    halves = [spread(mine), spread(exchange(mine, "row", n_row, top))]

    col_blocks = features.shape[0] // BLK
    row_total = col_blocks * n_col // n_row
    per = row_total // n_col
    slots = block_codes.shape[1]
    row_block, col_block = block_codes // col_blocks, block_codes % col_blocks
    owner = (row_block // per) ^ c
    live = lax.broadcasted_iota(jnp.int32, (1, slots), 1) < block_count
    source = col_block * LANES
    orders = [col_bits[1:] + col_bits[:1], col_bits]
    targets = []
    for order in orders:
        place = sum(((owner >> bit) & 1) << (len(order) - 1 - k) for k, bit in enumerate(order))
        targets.append(jnp.where(live, place * per + row_block % per, row_total) * PAIR)

    blocks = relayout(block_values[0])
    sums = [product(block_count, source, t, blocks, ft, row_total) for t, ft in zip(targets, halves)]

    for k in range(len(col_bits)):
        for i, order in enumerate(orders):
            keep, send = sums[i]
            got = exchange(send, "col", n_col, order[k])
            if k < len(col_bits) - 1:
                half = keep.shape[0] // 2
                total = keep + got.astype(jnp.float32)
                sums[i] = (total[:half], total[half:].astype(jnp.bfloat16))
            else:
                sums[i] = (keep, got)

    pieces = weight.reshape(n_row, -1, weight.shape[1])[jnp.arange(n_row) ^ r]
    pieces = pieces.reshape(2, BLK, weight.shape[1])
    zero = jnp.zeros_like(pieces)
    even = jnp.concatenate([pieces, zero], axis=1).reshape(2 * LANES, -1)
    odd = jnp.concatenate([zero, pieces], axis=1).reshape(2 * LANES, -1)
    return layer(*sums[0], *sums[1], even, odd, bias[None, :])


def solution(mesh):
    in_specs = (P("col", "row"), P("row", "col"), P("row", "col"), P("row", "col", None), P(), P())
    out_specs = P(("row", "col"), None)
    body = functools.partial(shards, mesh.shape["row"], mesh.shape["col"])
    return jax.shard_map(body, mesh=mesh, in_specs=in_specs, out_specs=out_specs, check_vma=False)
```

time: 215 us -> 78.6 us (0.37)
  waiting for transfers between devices: 96.7 us -> 23.8 us
  other arithmetic: 59.4 us -> 3.17 us
  Pallas kernels: 0 us -> 25.9 us
  local copies, waits for them, and re-layouts: 30.4 us -> 5.35 us
  starting transfers between devices: 0.04 us -> 19.5 us
  between operations: 14.1 us -> 0.83 us
  matrix products: 13.1 us -> 0 us
    reduce_scatter x1 -> x0, waiting for transfers between devices: 88.7 us -> none  [shards(): lax.psum_scatter(partial_rows, 'col', scatter_dimension=0, tiled=True)]
    scatter-add x1 -> x0, other arithmetic: 59.3 us -> none  [shards(): jax.ops.segment_sum(products, row_block, num_segments=row_total)]
    pallas_call x0 -> x4, Pallas kernels: none -> 25.9 us  [the longest x1 14.5 us: relayout(): pl.pallas_call(relayout_kernel, grid=(slots // GROUP,), in_specs=[pl.Bloc...]
    ppermute x0 -> x9, waiting for transfers between devices: none -> 23.8 us  [exchange(): return lax.ppermute(x, axis, [(i, i ^ 1 << bit) for i in range(size)])]
    ppermute x0 -> x9, starting transfers between devices: none -> 19.5 us  [exchange(): return lax.ppermute(x, axis, [(i, i ^ 1 << bit) for i in range(size)])]
    dot_general x2 -> x0, matrix products: 13.1 us -> none  [the longest x1 11 us: shards(): jnp.einsum('bij,bjf->bif', blocks, picked, preferred_element_type=jnp.flo...]
    gather x1, local copies, waits for them, and re-layouts: 13.3 us -> 0.55 us  [shards(): pieces = weight.reshape(n_row, -1, weight.shape[1])[jnp.arange(n_row) ^ r]]
    another operation x1 -> x0, local copies, waits for them, and re-layouts: 9.56 us -> none  [shards(): blocks = block_values[0].reshape(slots, BLK, BLK)]
  transfers between devices with their start and end apart: 2 -> 9, of which waited for: 2 -> 4; matrix products, arithmetic and copies ran while one was open for 6% -> 8% of each run, Pallas kernels for 0% -> 30%
where the time goes in v1:
time: 78.6 us; the launch traced here: 78.5 us
  Pallas kernels  25.9 us (33%)
  waiting for transfers between devices  23.8 us (30%)
  starting transfers between devices  19.5 us (25%)
  local copies, waits for them, and re-layouts  5.35 us (7%)
  other arithmetic  3.17 us (4%)
  between operations  0.83 us (1%)
    ppermute x9, waiting for transfers between devices, exchange(): return lax.ppermute(x, axis, [(i, i ^ 1 << bit) for i in range(size)])  23.8 us
    ppermute x9, starting transfers between devices, exchange(): return lax.ppermute(x, axis, [(i, i ^ 1 << bit) for i in range(size)])  19.5 us
    pallas_call x1, Pallas kernels, relayout(): pl.pallas_call(relayout_kernel, grid=(slots // GROUP,), in_specs=[pl.Bloc...  14.5 us
    pallas_call x2, Pallas kernels, product(): pl.pallas_call(product_kernel, in_specs=[smem, smem, smem, vmem, vmem], o...  8.96 us
    unnamed x10, local copies, waits for them, and re-layouts  2.56 us
    pallas_call x1, Pallas kernels, layer(): pl.pallas_call(layer_kernel, out_shape=jax.ShapeDtypeStruct((2 * rows, ev...  2.42 us
    add x4, other arithmetic, shards(): total = keep + got.astype(jnp.float32)  2.35 us
  transfers between devices with their start and end apart: 9, of which 4 were waited for; matrix products, arithmetic and copies ran while one was open for 8% of the time, Pallas kernels for 30%

profile of v1, /device:TPU:0, one launch (start us, length us, event | category | flops | bytes accessed | tf_op | source)
XLA Modules:
  0.0 78.5 jit_solution(4594617394737298446)
XLA Ops:
  0.0 0.5 collective-permute-start
  0.5 2.6 %collective-permute-start.4 = (bf16[32,4096]{1,0:T(8,128)(2,1)}, bf16[32,4096]{1,0:T(8,128)(2,1)S(1)}, u32[]{:S(2)}, u32[]{:S(2)}) collective-permute-start(bf16[32,4096]{1,0:T(8,128)(2,1)} %bitcast.18), channel_id=1, source_target_pairs={{0,16},{8,24},{16,0},{24,8},{1,17},{9,25},{17,1},{25,9},{2,18},{10... | collective-permute-start | bytes 786440 | tf_op jit(solution)/shard_map/ppermute | solution.py:130
  3.7 0.7 and_select_fusion.2
  4.4 0.0 copy-start.2
  4.5 14.5 %relayout.1.blocks_ref = bf16[12288,128]{1,0:T(8,128)(2,1)} custom-call(bf16[384,4096]{1,0:T(8,128)(2,1)} %bitcast.13), custom_call_target="tpu_custom_call" | custom-call | bytes 6291456 | tf_op jit(solution)/shard_map/relayout/pallas_call | solution.py:27
  18.9 0.0 collective-permute-done.4
  19.0 0.2 collective-permute-start.5
  19.2 0.0 collective-permute-done
  19.2 1.9 %copy-done.1 = bf16[12288,128]{1,0:T(8,128)(2,1)S(1)} copy-done((bf16[12288,128]{1,0:T(8,128)(2,1)S(1)}, bf16[12288,128]{1,0:T(8,128)(2,1)}, u32[]{:S(2)}) %copy-start.1) | copy-done | bytes 3145752
  21.1 4.5 %product.2 = (f32[2048,128]{1,0:T(8,128)S(1)}, bf16[2048,128]{1,0:T(8,128)(2,1)S(1)}) custom-call(s32[1,1]{1,0:T(1,128)} %copy.7.count_ref, s32[1,384]{1,0:T(1,128)S(1)} %fusion.2.source_ref, s32[1,384]{1,0:T(1,128)S(1)} %fusion.target_ref, bf16[12288,128]{1,0:T(8,128)(2,1)S(1)} %copy-done.1, bf16[64,4096]{1,0:T(8,128)(2,1)S(1)} %pad_maximum_fusion.ft_ref), custom_call_target="tpu_custom_call" | custom-call | flops 402653184 | bytes 6291456 | tf_op jit(solution)/shard_map/product/pallas_call | solution.py:81
  25.6 5.4 %collective-permute-start.1 = (bf16[2048,128]{1,0:T(8,128)(2,1)S(1)}, bf16[2048,128]{1,0:T(8,128)(2,1)}, u32[]{:S(2)}, u32[]{:S(2)}) collective-permute-start(bf16[2048,128]{1,0:T(8,128)(2,1)S(1)} %get-tuple-element.10), channel_id=1, source_target_pairs={{0,2},{1,3},{2,0},{3,1},{4,6},{5,7},{6,4},{7,5},{8,10},{9,11},{10,... | collective-permute-start | bytes 1572872 | tf_op jit(solution)/shard_map/ppermute | solution.py:130
  31.0 0.0 collective-permute-done.5
  31.1 4.5 %product.3 = (f32[2048,128]{1,0:T(8,128)S(1)}, bf16[2048,128]{1,0:T(8,128)(2,1)S(1)}) custom-call(s32[1,1]{1,0:T(1,128)} %copy.7.count_ref, s32[1,384]{1,0:T(1,128)S(1)} %fusion.2.source_ref, s32[1,384]{1,0:T(1,128)S(1)} %get-tuple-element.13.target_ref, bf16[12288,128]{1,0:T(8,128)(2,1)S(1)} %copy-done.1, bf16[64,4096]{1,0:T(8,128)(2,1)S(1)} %pad_maximum_fusion.1.ft_ref), custom_call_target="tpu_custom_call" | custom-call | flops 402653184 | bytes 6291456 | tf_op jit(solution)/shard_map/product/pallas_call | solution.py:81
  35.6 0.1 collective-permute-start.6
  35.6 5.2 %collective-permute-done.1 = bf16[2048,128]{1,0:T(8,128)(2,1)} collective-permute-done((bf16[2048,128]{1,0:T(8,128)(2,1)S(1)}, bf16[2048,128]{1,0:T(8,128)(2,1)}, u32[]{:S(2)}, u32[]{:S(2)}) %collective-permute-start.1) | collective-permute-done | bytes 524320 | tf_op jit(solution)/shard_map/ppermute | solution.py:130
  40.9 1.1 %convert_add_fusion.1 = f32[2048,128]{1,0:T(8,128)S(1)} fusion(f32[2048,128]{1,0:T(8,128)S(1)} %get-tuple-element.9, bf16[2048,128]{1,0:T(8,128)(2,1)} %collective-permute-done.1), kind=kLoop, calls=%fused_computation.2 | loop fusion | flops 524288 | bytes 2621440 | tf_op jit(solution)/shard_map/add | solution.py:169
  42.1 9.3 %collective-permute-start.2 = (bf16[1024,128]{1,0:T(8,128)(2,1)S(1)}, bf16[1024,128]{1,0:T(8,128)(2,1)S(1)}, u32[]{:S(2)}, u32[]{:S(2)}) collective-permute-start(bf16[1024,128]{1,0:T(8,128)(2,1)S(1)} %slice.53), channel_id=1, source_target_pairs={{0,4},{1,5},{2,6},{3,7},{4,0},{5,1},{6,2},{7,3},{8,12},{9,13},{10,... | collective-permute-start | bytes 786440 | tf_op jit(solution)/shard_map/ppermute | solution.py:130
  51.4 0.0 collective-permute-done.6
  51.4 1.1 %convert_add_fusion = f32[2048,128]{1,0:T(8,128)S(1)} fusion(f32[2048,128]{1,0:T(8,128)S(1)} %get-tuple-element.11, bf16[2048,128]{1,0:T(8,128)(2,1)} %collective-permute-done.6), kind=kLoop, calls=%fused_computation.1 | loop fusion | flops 524288 | bytes 2621440 | tf_op jit(solution)/shard_map/add | solution.py:169
  52.6 1.2 %collective-permute-start.7 = (bf16[1024,128]{1,0:T(8,128)(2,1)S(1)}, bf16[1024,128]{1,0:T(8,128)(2,1)S(1)}, u32[]{:S(2)}, u32[]{:S(2)}) collective-permute-start(bf16[1024,128]{1,0:T(8,128)(2,1)S(1)} %slice.52), channel_id=1, source_target_pairs={{0,2},{1,3},{2,0},{3,1},{4,6},{5,7},{6,4},{7,5},{8,10},{9,11},{10,... | collective-permute-start | bytes 786440 | tf_op jit(solution)/shard_map/ppermute | solution.py:130
  53.8 7.6 %collective-permute-done.2 = bf16[1024,128]{1,0:T(8,128)(2,1)S(1)} collective-permute-done((bf16[1024,128]{1,0:T(8,128)(2,1)S(1)}, bf16[1024,128]{1,0:T(8,128)(2,1)S(1)}, u32[]{:S(2)}, u32[]{:S(2)}) %collective-permute-start.2) | collective-permute-done | bytes 262176 | tf_op jit(solution)/shard_map/ppermute | solution.py:130
  61.4 0.1 collective-permute-start.3
  61.5 5.4 %collective-permute-done.7 = bf16[1024,128]{1,0:T(8,128)(2,1)S(1)} collective-permute-done((bf16[1024,128]{1,0:T(8,128)(2,1)S(1)}, bf16[1024,128]{1,0:T(8,128)(2,1)S(1)}, u32[]{:S(2)}, u32[]{:S(2)}) %collective-permute-start.7) | collective-permute-done | bytes 262176 | tf_op jit(solution)/shard_map/ppermute | solution.py:130
  67.0 0.1 collective-permute-start.8
  67.1 0.6 gather_fusion
  67.6 0.7 fusion.6
  68.3 0.7 slice.40.keep0
  69.1 0.7 slice.44.keep1
  69.8 0.0 collective-permute-done.3.got0
  69.8 5.6 %collective-permute-done.8.got1 = bf16[512,128]{1,0:T(8,128)(2,1)S(1)} collective-permute-done((bf16[512,128]{1,0:T(8,128)(2,1)S(1)}, bf16[512,128]{1,0:T(8,128)(2,1)S(1)}, u32[]{:S(2)}, u32[]{:S(2)}) %collective-permute-start.8) | collective-permute-done | bytes 131104 | tf_op jit(solution)/shard_map/ppermute | solution.py:130
  75.4 0.7 copy-done.4
  76.1 2.4 %layer.1 = bf16[1024,256]{1,0:T(8,128)(2,1)} custom-call(f32[512,128]{1,0:T(8,128)} %slice.40.keep0, bf16[512,128]{1,0:T(8,128)(2,1)} %copy-done.3, f32[512,128]{1,0:T(8,128)} %slice.44.keep1, bf16[512,128]{1,0:T(8,128)(2,1)} %copy-done.4, bf16[256,256]{1,0:T(8,128)(2,1)} %bitcast.15, bf16[256,256]{1,0:T(8,128)(2,1)} %bitcast.14, f32[1,256]{1,0:T(1,128)} %bitcast.20), custom_call_target="tpu_custom_call" | custom-call | tf_op jit(solution)/shard_map/layer/pallas_call | solution.py:117
  (20 shorter events, 0.3 us)
Async XLA Ops:
  0.0 67.1 %copy-start = (bf16[128,256]{1,0:T(8,128)(2,1)S(1)}, bf16[128,256]{1,0:T(8,128)(2,1)}, u32[]{:S(2)}) copy-start(bf16[128,256]{1,0:T(8,128)(2,1)} %param.10) | copy-start | bytes 196612
  0.0 19.2 %collective-permute-start = (bf16[32,4096]{1,0:T(8,128)(2,1)}, bf16[32,4096]{1,0:T(8,128)(2,1)S(1)}, u32[]{:S(2)}, u32[]{:S(2)}) collective-permute-start(bf16[32,4096]{1,0:T(8,128)(2,1)} %bitcast.17), channel_id=1, source_target_pairs={{0,8},{8,0},{16,24},{24,16},{1,9},{9,1},{17,25},{25,17},{2,10},{10... | collective-permute-start | bytes 786440 | tf_op jit(solution)/shard_map/ppermute | solution.py:130
  0.5 18.5 %collective-permute-start.4 = (bf16[32,4096]{1,0:T(8,128)(2,1)}, bf16[32,4096]{1,0:T(8,128)(2,1)S(1)}, u32[]{:S(2)}, u32[]{:S(2)}) collective-permute-start(bf16[32,4096]{1,0:T(8,128)(2,1)} %bitcast.18), channel_id=1, source_target_pairs={{0,16},{8,24},{16,0},{24,8},{1,17},{9,25},{17,1},{25,9},{2,18},{10... | collective-permute-start | bytes 786440 | tf_op jit(solution)/shard_map/ppermute | solution.py:130
  4.4 14.7 %copy-start.2 = (bf16[4096,32]{0,1:T(8,128)(2,1)S(1)}, bf16[4096,32]{0,1:T(8,128)(2,1)}, u32[]{:S(2)}) copy-start(bf16[4096,32]{0,1:T(8,128)(2,1)} %param.6) | copy-start | bytes 786436
  19.0 12.1 %collective-permute-start.5 = (bf16[32,4096]{1,0:T(8,128)(2,1)S(1)}, bf16[32,4096]{1,0:T(8,128)(2,1)S(1)}, u32[]{:S(2)}, u32[]{:S(2)}) collective-permute-start(bf16[32,4096]{1,0:T(8,128)(2,1)S(1)} %collective-permute-done.4), channel_id=1, source_target_pairs={{0,8},{8,0},{16,24},{24,16},{1,9},{9,1},{17,25},{25,17},{2,10},{10... | collective-permute-start | bytes 786440 | tf_op jit(solution)/shard_map/ppermute | solution.py:130
  19.2 1.9 %copy-start.1 = (bf16[12288,128]{1,0:T(8,128)(2,1)S(1)}, bf16[12288,128]{1,0:T(8,128)(2,1)}, u32[]{:S(2)}) copy-start(bf16[12288,128]{1,0:T(8,128)(2,1)} %relayout.1.blocks_ref) | copy-start | bytes 9437188
  25.6 15.3 %collective-permute-start.1 = (bf16[2048,128]{1,0:T(8,128)(2,1)S(1)}, bf16[2048,128]{1,0:T(8,128)(2,1)}, u32[]{:S(2)}, u32[]{:S(2)}) collective-permute-start(bf16[2048,128]{1,0:T(8,128)(2,1)S(1)} %get-tuple-element.10), channel_id=1, source_target_pairs={{0,2},{1,3},{2,0},{3,1},{4,6},{5,7},{6,4},{7,5},{8,10},{9,11},{10,... | collective-permute-start | bytes 1572872 | tf_op jit(solution)/shard_map/ppermute | solution.py:130
  35.6 15.8 %collective-permute-start.6 = (bf16[2048,128]{1,0:T(8,128)(2,1)S(1)}, bf16[2048,128]{1,0:T(8,128)(2,1)}, u32[]{:S(2)}, u32[]{:S(2)}) collective-permute-start(bf16[2048,128]{1,0:T(8,128)(2,1)S(1)} %get-tuple-element.12), channel_id=1, source_target_pairs={{0,1},{1,0},{2,3},{3,2},{4,5},{5,4},{6,7},{7,6},{8,9},{9,8},{10,11... | collective-permute-start | bytes 1572872 | tf_op jit(solution)/shard_map/ppermute | solution.py:130
  42.1 19.3 %collective-permute-start.2 = (bf16[1024,128]{1,0:T(8,128)(2,1)S(1)}, bf16[1024,128]{1,0:T(8,128)(2,1)S(1)}, u32[]{:S(2)}, u32[]{:S(2)}) collective-permute-start(bf16[1024,128]{1,0:T(8,128)(2,1)S(1)} %slice.53), channel_id=1, source_target_pairs={{0,4},{1,5},{2,6},{3,7},{4,0},{5,1},{6,2},{7,3},{8,12},{9,13},{10,... | collective-permute-start | bytes 786440 | tf_op jit(solution)/shard_map/ppermute | solution.py:130
  52.6 14.3 %collective-permute-start.7 = (bf16[1024,128]{1,0:T(8,128)(2,1)S(1)}, bf16[1024,128]{1,0:T(8,128)(2,1)S(1)}, u32[]{:S(2)}, u32[]{:S(2)}) collective-permute-start(bf16[1024,128]{1,0:T(8,128)(2,1)S(1)} %slice.52), channel_id=1, source_target_pairs={{0,2},{1,3},{2,0},{3,1},{4,6},{5,7},{6,4},{7,5},{8,10},{9,11},{10,... | collective-permute-start | bytes 786440 | tf_op jit(solution)/shard_map/ppermute | solution.py:130
  61.4 8.4 %collective-permute-start.3 = (bf16[512,128]{1,0:T(8,128)(2,1)S(1)}, bf16[512,128]{1,0:T(8,128)(2,1)S(1)}, u32[]{:S(2)}, u32[]{:S(2)}) collective-permute-start(bf16[512,128]{1,0:T(8,128)(2,1)S(1)} %slice.55), channel_id=1, source_target_pairs={{0,1},{1,0},{2,3},{3,2},{4,5},{5,4},{6,7},{7,6},{8,9},{9,8},{10,11... | collective-permute-start | bytes 393224 | tf_op jit(solution)/shard_map/ppermute | solution.py:130
  67.0 8.5 %collective-permute-start.8 = (bf16[512,128]{1,0:T(8,128)(2,1)S(1)}, bf16[512,128]{1,0:T(8,128)(2,1)S(1)}, u32[]{:S(2)}, u32[]{:S(2)}) collective-permute-start(bf16[512,128]{1,0:T(8,128)(2,1)S(1)} %slice.54), channel_id=1, source_target_pairs={{0,4},{1,5},{2,6},{3,7},{4,0},{5,1},{6,2},{7,3},{8,12},{9,13},{10,... | collective-permute-start | bytes 393224 | tf_op jit(solution)/shard_map/ppermute | solution.py:130
  69.8 5.6 %copy-start.3 = (bf16[512,128]{1,0:T(8,128)(2,1)}, bf16[512,128]{1,0:T(8,128)(2,1)S(1)}, u32[]{:S(2)}) copy-start(bf16[512,128]{1,0:T(8,128)(2,1)S(1)} %collective-permute-done.3.got0) | copy-start | bytes 393220
  75.4 0.7 copy-start.4
